TPU v7x, 32 devices: a whole 2x2x4 slice. The times are simulated.
32 devices in a mesh: inp: 4 (over z), tm: 8 (over y, x, core).
Axes of the slice: x: 2, y: 2, z: 4, core: 2. Of those that a mesh axis runs over, the one named last changes fastest.
Arguments:
- samples: bfloat16 [512, 512, 1024], P('inp', 'tm'), may hold values from -6 to 6
- eq_gain: float32 [512, 512], P(None, 'inp'), may hold values from 0.5 to 2
Outputs:
- visibilities: float32 [512, 2, 512, 512], P(('inp', 'tm'))
All inputs are finite; a program needn't handle non-finite values.
Results may differ from a plain program's by a relative error of at most 0.0033.
Values may be sent and summed in bfloat16 or wider, within the bound.
A program may use at most 256 MiB of HBM per device.

v0:
```python
import math

import jax
import jax.numpy as jnp
from jax import lax
from jax.sharding import PartitionSpec as P

TAPS = 4


def passed_along(array, axis, by):
    devices = lax.axis_size(axis)
    pairs = [(i, i + by) for i in range(devices) if 0 <= i + by < devices]
    return lax.ppermute(array, axis, pairs)


def window_table(taps, nfft):
    position = jnp.arange(taps * nfft, dtype=jnp.int32).astype(jnp.float32) + 0.5
    shape_part = jnp.sinc(position / nfft - taps / 2.0)
    taper = 0.5 - 0.5 * jnp.cos(position * (2.0 * math.pi / (taps * nfft)))
    return (shape_part * taper).reshape(taps, nfft)


def fourier_table(channels, nfft):
    chan = jnp.arange(channels, dtype=jnp.int32)
    point = jnp.arange(nfft, dtype=jnp.int32)
    phase = (chan[:, None] * point[None, :] % nfft).astype(jnp.float32) * (2.0 * math.pi / nfft)
    scale = 1.0 / math.sqrt(nfft)
    table = jnp.stack([jnp.cos(phase) * scale, -jnp.sin(phase) * scale], axis=1)
    return table.reshape(2 * channels, nfft).astype(jnp.bfloat16)


def correlate(blocks, frames_all):
    groups_in = blocks.shape[0]
    count = blocks.shape[2]
    local_inputs = blocks.shape[4]
    inputs_all = groups_in * local_inputs
    gram = jnp.einsum("ptcraf,qtcsbf->crpasqb", blocks, blocks, preferred_element_type=jnp.float32)
    gram = gram.reshape(count, 2, inputs_all, 2, inputs_all)
    real_part = (gram[:, 0, :, 0, :] + gram[:, 1, :, 1, :]) / frames_all
    imag_part = (gram[:, 1, :, 0, :] - gram[:, 0, :, 1, :]) / frames_all
    return jnp.stack([real_part, imag_part], axis=1)


def on_device(samples, eq_gain):
    local_inputs = samples.shape[0]
    local_frames = samples.shape[1]
    nfft = samples.shape[2]
    channels = nfft // 2
    n_inp = lax.axis_size("inp")
    n_time = lax.axis_size("tm")
    groups = n_inp * n_time
    chan_dev = channels // groups
    frames_all = n_time * local_frames
    tail = samples[:, local_frames - (TAPS - 1) :, :]
    before = passed_along(tail, "tm", 1)
    padded = jnp.concatenate([before, samples], axis=1)
    window = window_table(TAPS, nfft)
    filtered = jnp.zeros((local_inputs, local_frames, nfft), jnp.float32)
    for tap in range(TAPS):
        filtered = filtered + window[tap] * padded[:, tap : tap + local_frames, :].astype(
            jnp.float32
        )
    filtered = filtered.astype(jnp.bfloat16)
    table = fourier_table(channels, nfft)
    spectra = lax.dot_general(
        table, filtered, (((1,), (2,)), ((), ())), preferred_element_type=jnp.float32
    )
    spectra = spectra.reshape(channels, 2, local_inputs, local_frames) * eq_gain[:, None, :, None]
    spectra = spectra.astype(jnp.bfloat16)
    parcel = spectra.reshape(1, groups, chan_dev, 2, local_inputs, local_frames)
    arrived = lax.all_to_all(parcel, ("inp", "tm"), split_axis=1, concat_axis=0, tiled=True)
    count = arrived.shape[2]
    blocks = arrived.reshape(n_inp, n_time, count, 2, local_inputs, local_frames)
    return correlate(blocks, frames_all)


def solution(mesh):
    placed = (P("inp", "tm", None), P(None, "inp"))
    return jax.shard_map(
        on_device,
        mesh=mesh,
        in_specs=placed,
        out_specs=P(("inp", "tm"), None, None, None),
        check_vma=False,
    )
```

profile of v0, /device:TPU:16, one launch (start us, length us, event | category | flops | bytes accessed | tf_op | source)
XLA Modules:
  0.0 740.8 jit_solution(16562488204710347606)
XLA Ops:
  0.0 2.1 slice.41
  2.1 0.3 copy.33
  2.5 1.8 collective-permute-start
  4.3 0.1 fusion.23
  4.4 8.6 %multiply_convert_fusion.1 = (bf16[512,1,1024]{2,0,1:T(8,128)(2,1)S(1)}, bf16[512,1,1024]{2,0,1:T(8,128)(2,1)S(1)}) fusion(), kind=kLoop, calls=%fused_computation.32 | loop fusion | flops 9961472 | bytes 2097152 | tf_op jit(solution)/shard_map/convert.1
  12.9 0.0 collective-permute-done
  12.9 0.7 copy.15
  13.6 0.0 copy-start
  13.6 35.4 %add_convert_fusion = bf16[128,64,1024]{2,1,0:T(8,128)(2,1)} fusion(bf16[128,64,1024]{2,1,0:T(8,128)(2,1)} %param.2, bf16[128,3,1024]{2,1,0:T(4,128)(2,1)S(1)} %copy.15, f32[1024]{0:T(1024)S(1)} %get-tuple-element.6, f32[1024]{0:T(1024)S(1)} %get-tuple-element.7, f32[1024]{0:T(1024)S(1)} %get-tuple-element.8, f32[1024]{0:T(1024)S(1)} %get-tuple-element.5), kind=kLoop, calls=%fused_computation.2 | loop fusion | flops 176160768 | bytes 34357248 | tf_op jit(solution)/shard_map/convert_element_type | solution.py:64
  49.0 0.0 copy-done
  49.0 36.0 %multiply_convert_fusion = bf16[512,2,128,64]{2,0,3,1:T(8,128)(2,1)S(1)} fusion(bf16[128,64,1024]{2,1,0:T(8,128)(2,1)} %add_convert_fusion, f32[512,128]{1,0:T(8,128)S(1)} %copy-done, bf16[512,1,1024]{2,0,1:T(8,128)(2,1)S(1)} %get-tuple-element.9, bf16[512,1,1024]{2,0,1:T(8,128)(2,1)S(1)} %get-tuple-element.10), kind=kOutput, calls=%fused_computation.1 | convolution fusion | flops 17200840704 | bytes 35913728 | tf_op jit(solution)/shard_map/dot_general | solution.py:66
  85.0 36.7 %copy.17 = bf16[1,32,16,2,128,64]{4,5,3,2,0,1:T(8,128)(2,1)S(1)} copy(bf16[1,32,16,2,128,64]{4,2,1,5,3,0:T(8,128)(2,1)S(1)} %bitcast.39) | data formatting | bytes 33554432 | tf_op jit(solution)/shard_map/reshape | solution.py:71
  121.7 370.4 %all_to_all.4 = bf16[1,32,16,2,128,64]{4,5,3,2,0,1:T(8,128)(2,1)} all-to-all(bf16[1,32,16,2,128,64]{4,5,3,2,0,1:T(8,128)(2,1)S(1)} %copy.17), channel_id=1, replica_groups=mesh['inp'=4,'tm'=8] {'inp','tm'}, dimensions={1} | all-to-all | bytes 33554432 | tf_op jit(solution)/shard_map/all_to_all | solution.py:72
  492.1 36.1 %convolution_bitcast_fusion = f32[16,2,4,128,2,4,128]{3,6,1,2,4,5,0:T(8,128)} fusion(bf16[4,8,16,2,128,64,1,1]{4,5,3,2,1,0,7,6:T(8,128)(2,1)} %bitcast.38), kind=kOutput, calls=%fused_computation.5 | convolution fusion | flops 17179869184 | bytes 83886080 | tf_op jit(solution)/shard_map/ptcraf,qtcsbf->crpasqb/dot_general | solution.py:38
  528.2 75.4 %copy.20 = f32[16,2,4,128,2,4,128]{6,5,3,2,4,1,0:T(4,128)} copy(f32[16,2,4,128,2,4,128]{3,6,1,2,4,5,0:T(8,128)} %convolution_bitcast_fusion) | data formatting | bytes 134217728 | tf_op jit(solution)/shard_map/ptcraf,qtcsbf->crpasqb/transpose | solution.py:38
  603.6 77.6 %reshape.153 = f32[16,2,512,2,512]{4,2,3,1,0:T(8,128)} reshape(f32[16,2,4,128,2,4,128]{6,5,3,2,4,1,0:T(4,128)} %copy.20) | data formatting | bytes 134217728 | tf_op jit(solution)/shard_map/reshape | solution.py:39
  681.2 17.6 %fusion.3 = f32[16,1,512,512]{3,2,0,1:T(8,128)} fusion(f32[16,2,512,2,512]{4,2,3,1,0:T(8,128)} %reshape.153), kind=kLoop, calls=%fused_computation.12 | loop fusion | flops 8388608 | bytes 50331648 | tf_op jit(solution)/shard_map/div | solution.py:41
  698.8 17.6 %fusion.6 = f32[16,1,512,512]{3,2,0,1:T(8,128)} fusion(f32[16,2,512,2,512]{4,2,3,1,0:T(8,128)} %reshape.153), kind=kLoop, calls=%fused_computation.16 | loop fusion | flops 8388608 | bytes 50331648 | tf_op jit(solution)/shard_map/div | solution.py:40
  716.3 13.0 %pad_maximum_fusion = f32[16,2,512,512]{3,2,0,1:T(8,128)S(1)} fusion(f32[16,1,512,512]{3,2,0,1:T(8,128)} %fusion.3, f32[16,1,512,512]{3,2,0,1:T(8,128)} %fusion.6), kind=kLoop, calls=%fused_computation | loop fusion | flops 8388608 | bytes 67108864 | tf_op jit(solution)/shard_map/stack | solution.py:42
  729.4 11.4 %copy.24 = f32[16,2,512,512]{3,2,1,0:T(8,128)} copy(f32[16,2,512,512]{3,2,0,1:T(8,128)S(1)} %pad_maximum_fusion) | data formatting | bytes 67108864 | tf_op jit(solution)/shard_map/stack | solution.py:42
  (1 shorter events, 0.0 us)
Async XLA Ops:
  2.5 10.5 %collective-permute-start = (bf16[128,3,1024]{2,0,1:T(8,128)(2,1)S(1)}, bf16[128,3,1024]{2,0,1:T(8,128)(2,1)S(1)}, u32[]{:S(2)}, u32[]{:S(2)}) collective-permute-start(bf16[128,3,1024]{2,0,1:T(8,128)(2,1)S(1)} %copy.33), channel_id=1, source_target_pairs={{0,1},{1,2},{2,3},{3,4},{4,5},{5,6},{6,7},{8,9},{9,10},{10,11},{11... | collective-permute-start | bytes 2359304 | tf_op jit(solution)/shard_map/ppermute | solution.py:14
  13.6 35.4 %copy-start = (f32[512,128]{1,0:T(8,128)S(1)}, f32[512,128]{1,0:T(8,128)}, u32[]{:S(2)}) copy-start(f32[512,128]{1,0:T(8,128)} %param.3) | copy-start | bytes 786436
where the time goes:
time: 747 us; the launch traced here: 741 us
  blocking collectives  370 us (50%)
  local copies, waits for them, and re-layouts  204 us (27%)
  other arithmetic  92.2 us (12%)
  matrix products  72.1 us (10%)
    all_to_all x1, blocking collectives, on_device(): lax.all_to_all(parcel, ('inp', 'tm'), split_axis=1, concat_axis=0, tiled=...  370 us
    reshape x1, local copies, waits for them, and re-layouts, correlate(): gram = gram.reshape(count, 2, inputs_all, 2, inputs_all)  77.6 us
    transpose x1, local copies, waits for them, and re-layouts, correlate(): jnp.einsum('ptcraf,qtcsbf->crpasqb', blocks, blocks, preferred_element_ty...  75.4 us
    reshape x1, local copies, waits for them, and re-layouts, on_device(): parcel = spectra.reshape(1, groups, chan_dev, 2, local_inputs, local_frames)  36.7 us
    dot_general x1, matrix products, correlate(): jnp.einsum('ptcraf,qtcsbf->crpasqb', blocks, blocks, preferred_element_ty...  36.1 us
    dot_general x1, matrix products, on_device(): lax.dot_general(table, filtered, (((1,), (2,)), ((), ())), preferred_elem...  36 us
    convert_element_type x1, other arithmetic, on_device(): filtered = filtered.astype(jnp.bfloat16)  35.4 us
    div x1, other arithmetic, correlate(): imag_part = (gram[:, 1, :, 0, :] - gram[:, 0, :, 1, :]) / frames_all  17.6 us
  transfers between devices with their start and end apart: 1, of which 0 were waited for; matrix products, arithmetic and copies ran while one was open for 1% of the time, Pallas kernels for 0%

commit v1 on v0

--- a/solution.py
+++ b/solution.py
@@ -1,11 +1,17 @@
+import functools
 import math
 
 import jax
 import jax.numpy as jnp
+import numpy as np
 from jax import lax
+from jax.experimental import pallas as pl
+from jax.experimental.pallas import tpu as pltpu
 from jax.sharding import PartitionSpec as P
 
 TAPS = 4
+LANES = 128
+STEP = 16
 
 
 def passed_along(array, axis, by):
@@ -15,22 +21,22 @@
 
 
 def window_table(taps, nfft):
-    position = jnp.arange(taps * nfft, dtype=jnp.int32).astype(jnp.float32) + 0.5
-    shape_part = jnp.sinc(position / nfft - taps / 2.0)
-    taper = 0.5 - 0.5 * jnp.cos(position * (2.0 * math.pi / (taps * nfft)))
-    return (shape_part * taper).reshape(taps, nfft)
+    position = np.arange(taps * nfft, dtype=np.float64) + 0.5
+    shape_part = np.sinc(position / nfft - taps / 2.0)
+    taper = 0.5 - 0.5 * np.cos(position * (2.0 * math.pi / (taps * nfft)))
+    return (shape_part * taper).reshape(taps, nfft).astype(np.float32)
 
 
 def fourier_table(channels, nfft):
-    chan = jnp.arange(channels, dtype=jnp.int32)
-    point = jnp.arange(nfft, dtype=jnp.int32)
-    phase = (chan[:, None] * point[None, :] % nfft).astype(jnp.float32) * (2.0 * math.pi / nfft)
+    chan = np.arange(channels)
+    point = np.arange(nfft)
+    phase = (chan[:, None] * point[None, :] % nfft) * (2.0 * math.pi / nfft)
     scale = 1.0 / math.sqrt(nfft)
-    table = jnp.stack([jnp.cos(phase) * scale, -jnp.sin(phase) * scale], axis=1)
-    return table.reshape(2 * channels, nfft).astype(jnp.bfloat16)
-
-
-def correlate(blocks, frames_all):
+    table = np.stack([np.cos(phase) * scale, -np.sin(phase) * scale], axis=1)
+    return table.reshape(2 * channels, nfft).astype(np.float32).astype(jnp.bfloat16)
+
+
+def correlate_einsum(blocks, frames_all):
     groups_in = blocks.shape[0]
     count = blocks.shape[2]
     local_inputs = blocks.shape[4]
@@ -42,10 +48,8 @@
     return jnp.stack([real_part, imag_part], axis=1)
 
 
-def on_device(samples, eq_gain):
-    local_inputs = samples.shape[0]
-    local_frames = samples.shape[1]
-    nfft = samples.shape[2]
+def plain_plan(samples, eq_gain):
+    local_inputs, local_frames, nfft = samples.shape
     channels = nfft // 2
     n_inp = lax.axis_size("inp")
     n_time = lax.axis_size("tm")
@@ -62,7 +66,7 @@
             jnp.float32
         )
     filtered = filtered.astype(jnp.bfloat16)
-    table = fourier_table(channels, nfft)
+    table = jnp.asarray(fourier_table(channels, nfft))
     spectra = lax.dot_general(
         table, filtered, (((1,), (2,)), ((), ())), preferred_element_type=jnp.float32
     )
@@ -72,7 +76,250 @@
     arrived = lax.all_to_all(parcel, ("inp", "tm"), split_axis=1, concat_axis=0, tiled=True)
     count = arrived.shape[2]
     blocks = arrived.reshape(n_inp, n_time, count, 2, local_inputs, local_frames)
-    return correlate(blocks, frames_all)
+    return correlate_einsum(blocks, frames_all)
+
+
+def spread_kernel(
+    n_inp, n_time,
+    x_hbm, before_ref, gain_ref, table_ref, window_ref,
+    recv_hbm,
+    xbuf, turned, taps_buf, history, filt, freq, send,
+    load_sem, send_sem, recv_sem, own_sem,
+):
+    groups = n_inp * n_time
+    inputs, frames, nfft = x_hbm.shape
+    rows_all = table_ref.shape[0]
+    rows_plane = rows_all // n_inp
+    rows_dev = rows_all // groups
+    pitch = freq.shape[0] // STEP
+    steps = frames // STEP
+    tiles = nfft // LANES
+    z = lax.axis_index("inp")
+    t = lax.axis_index("tm")
+    me = z * n_time + t
+
+    def load(step, slot):
+        f0 = pl.multiple_of(step * STEP, STEP)
+        return pltpu.make_async_copy(
+            x_hbm.at[:, pl.ds(f0, STEP), :], xbuf.at[slot], load_sem.at[slot]
+        )
+
+    load(0, 0).start()
+    barrier = pltpu.get_barrier_semaphore()
+
+    @pl.loop(1, groups)
+    def _(s):
+        d = lax.rem(me + s, groups)
+        pl.semaphore_signal(
+            barrier, inc=1, device_id=(d // n_time, lax.rem(d, n_time)),
+            device_id_type=pl.DeviceIdType.MESH,
+        )
+
+    history[...] = before_ref[...].astype(jnp.float32)
+
+    def send_one(step, d_z, d_t):
+        f0 = pl.multiple_of(step * STEP, STEP)
+        d = d_z * n_time + d_t
+        r0 = pl.multiple_of(d * rows_dev, rows_dev)
+        pltpu.make_async_remote_copy(
+            src_ref=send.at[pl.ds(r0, rows_dev), pl.ds(f0, STEP), :],
+            dst_ref=recv_hbm.at[me, :, pl.ds(f0, STEP), :],
+            send_sem=send_sem.at[d],
+            recv_sem=recv_sem.at[me],
+            device_id=(d_z, d_t),
+            device_id_type=pl.DeviceIdType.MESH,
+        ).start()
+
+    def filter_step(slot):
+        @pl.loop(0, tiles)
+        def _(tile):
+            lanes = pl.ds(pl.multiple_of(tile * LANES, LANES), LANES)
+            turned[...] = (
+                xbuf[slot, :, :, lanes].astype(jnp.float32).reshape(inputs * STEP, LANES)
+            )
+            taps_buf[0 : TAPS - 1] = history[:, :, lanes]
+            for f in range(STEP):
+                taps_buf[TAPS - 1 + f] = turned[pl.ds(f, inputs, stride=STEP), :]
+            history[:, :, lanes] = taps_buf[STEP : STEP + TAPS - 1]
+            for f in range(STEP):
+                total = window_ref[0:1, lanes] * taps_buf[f]
+                for tap in range(1, TAPS):
+                    total = total + window_ref[tap : tap + 1, lanes] * taps_buf[f + tap]
+                filt[f * inputs : (f + 1) * inputs, lanes] = total.astype(jnp.bfloat16)
+
+    def transform(step, plane):
+        f0 = pl.multiple_of(step * STEP, STEP)
+        base = pl.multiple_of(plane * rows_plane, rows_plane)
+        width = 4
+
+        @pl.loop(0, STEP // width)
+        def _(j):
+            some = filt[pl.ds(pl.multiple_of(j * width * inputs, width * inputs), width * inputs), :]
+            got = lax.dot_general(
+                table_ref[pl.ds(base, rows_plane), :], some,
+                (((1,), (1,)), ((), ())), preferred_element_type=jnp.float32,
+            )
+            for w in range(width):
+                at = pl.multiple_of((j * width + w) * pitch, 8)
+                freq[pl.ds(at, rows_plane), :] = got[:, w * inputs : (w + 1) * inputs]
+
+        @pl.loop(0, rows_plane // 8)
+        def _(i):
+            for k in range(8):
+                row = i * 8 + k
+                chan = plane * (rows_plane // 2) + i * 4 + k // 2
+                value = freq[pl.ds(row, STEP, stride=pitch), :] * gain_ref[pl.ds(chan, 1), :]
+                send[base + row, pl.ds(f0, STEP), :] = value.astype(jnp.bfloat16)
+
+    far = lax.rem(z + 2, 4)
+    farther = 3 - z
+    near = z + 1 - 2 * lax.rem(z, 2)
+
+    @pl.loop(0, steps)
+    def _(step):
+        slot = lax.rem(step, 2)
+        load(step, slot).wait()
+
+        @pl.when(step + 1 < steps)
+        def _():
+            load(step + 1, 1 - slot).start()
+
+        filter_step(slot)
+        transform(step, far)
+
+        @pl.when(step == 0)
+        def _():
+            pl.semaphore_wait(barrier, groups - 1)
+
+        @pl.loop(0, n_time)
+        def _(s):
+            send_one(step, far, lax.rem(t + s, n_time))
+
+            @pl.when((step > 0) & (s > 0))
+            def _():
+                send_one(step - 1, z, lax.rem(t + s, n_time))
+
+        transform(step, near)
+        transform(step, farther)
+
+        @pl.loop(0, n_time)
+        def _(s):
+            send_one(step, farther, lax.rem(t + s, n_time))
+            send_one(step, near, lax.rem(t + s, n_time))
+
+        transform(step, z)
+
+    @pl.loop(1, n_time)
+    def _(s):
+        send_one(steps - 1, z, lax.rem(t + s, n_time))
+
+    own = pltpu.make_async_copy(
+        send.at[pl.ds(pl.multiple_of(me * rows_dev, rows_dev), rows_dev)], recv_hbm.at[me], own_sem
+    )
+    own.start()
+    own.wait()
+
+    @pl.loop(1, groups)
+    def _(s):
+        d = lax.rem(me + s, groups)
+        gone = send.at[pl.ds(pl.multiple_of(d * rows_dev, rows_dev), rows_dev)]
+        pltpu.make_async_copy(gone, gone, send_sem.at[d]).wait()
+        here = recv_hbm.at[d]
+        pltpu.make_async_copy(here, here, recv_sem.at[d]).wait()
+
+
+def spread(samples, before, eq_gain, n_inp, n_time):
+    inputs, frames, nfft = samples.shape
+    channels = nfft // 2
+    rows = 2 * channels
+    groups = n_inp * n_time
+    pitch = rows // n_inp + 8
+    vmem = pl.BlockSpec(memory_space=pltpu.VMEM)
+    anywhere = pl.BlockSpec(memory_space=pl.ANY)
+    return pl.pallas_call(
+        functools.partial(spread_kernel, n_inp, n_time),
+        out_shape=jax.ShapeDtypeStruct((groups, rows // groups, frames, inputs), jnp.bfloat16),
+        in_specs=[anywhere, vmem, vmem, vmem, vmem],
+        out_specs=anywhere,
+        scratch_shapes=[
+            pltpu.VMEM((2, inputs, STEP, nfft), jnp.bfloat16),
+            pltpu.VMEM((inputs * STEP, LANES), jnp.float32),
+            pltpu.VMEM((STEP + TAPS - 1, inputs, LANES), jnp.float32),
+            pltpu.VMEM((TAPS - 1, inputs, nfft), jnp.float32),
+            pltpu.VMEM((STEP * inputs, nfft), jnp.bfloat16),
+            pltpu.VMEM((STEP * pitch, LANES), jnp.float32),
+            pltpu.VMEM((rows, frames, inputs), jnp.bfloat16),
+            pltpu.SemaphoreType.DMA((2,)),
+            pltpu.SemaphoreType.DMA((groups,)),
+            pltpu.SemaphoreType.DMA((groups,)),
+            pltpu.SemaphoreType.DMA,
+        ],
+        compiler_params=pltpu.CompilerParams(
+            collective_id=0, has_side_effects=True, vmem_limit_bytes=56 * 1024 * 1024
+        ),
+        cost_estimate=pl.CostEstimate(
+            flops=2 * rows * nfft * inputs * frames,
+            bytes_accessed=4 * inputs * frames * nfft,
+            transcendentals=0,
+        ),
+        name="filter_transform_spread",
+    )(
+        samples, before, eq_gain,
+        jnp.asarray(fourier_table(channels, nfft)), jnp.asarray(window_table(TAPS, nfft)),
+    )
+
+
+def correlate_kernel(n_inp, scale, block_ref, out_ref):
+    sources, _, frames, inputs = block_ref.shape
+    n_time = sources // n_inp
+
+    def part(r):
+        pieces = [
+            block_ref[p * n_time : (p + 1) * n_time, r].reshape(n_time * frames, inputs)
+            for p in range(n_inp)
+        ]
+        return jnp.concatenate(pieces, axis=1)
+
+    real, imag = part(0), part(1)
+    real_t, imag_t = real.T, imag.T
+    right = jnp.concatenate([real, imag], axis=0)
+    left = jnp.concatenate([real_t, imag_t], axis=1)
+    out_ref[0, 0] = jnp.dot(left, right, preferred_element_type=jnp.float32) * scale
+    left = jnp.concatenate([imag_t, -real_t], axis=1)
+    out_ref[0, 1] = jnp.dot(left, right, preferred_element_type=jnp.float32) * scale
+
+
+def correlate(arrived, n_inp):
+    sources, rows, frames, inputs = arrived.shape
+    count = rows // 2
+    inputs_all = n_inp * inputs
+    frames_all = sources // n_inp * frames
+    return pl.pallas_call(
+        functools.partial(correlate_kernel, n_inp, 1.0 / frames_all),
+        grid=(count,),
+        out_shape=jax.ShapeDtypeStruct((count, 2, inputs_all, inputs_all), jnp.float32),
+        in_specs=[pl.BlockSpec((sources, 2, frames, inputs), lambda c: (0, c, 0, 0))],
+        out_specs=pl.BlockSpec((1, 2, inputs_all, inputs_all), lambda c: (c, 0, 0, 0)),
+        compiler_params=pltpu.CompilerParams(vmem_limit_bytes=48 * 1024 * 1024),
+        cost_estimate=pl.CostEstimate(
+            flops=count * 8 * inputs_all * inputs_all * frames_all,
+            bytes_accessed=arrived.size * 2 + count * 8 * inputs_all * inputs_all,
+            transcendentals=0,
+        ),
+        name="correlate",
+    )(arrived)
+
+
+def on_device(samples, eq_gain):
+    local_inputs, local_frames, nfft = samples.shape
+    n_inp = lax.axis_size("inp")
+    n_time = lax.axis_size("tm")
+    if local_inputs != LANES or n_inp != 4 or n_time != 8 or local_frames % STEP:
+        return plain_plan(samples, eq_gain)
+    tail = jnp.swapaxes(samples[:, local_frames - (TAPS - 1) :, :], 0, 1)
+    before = passed_along(tail, "tm", 1)
+    arrived = spread(samples, before, eq_gain, n_inp, n_time)
+    return correlate(arrived, n_inp)
 
 
 def solution(mesh):

time: 747 us -> 427 us (0.57)
  Pallas kernels: 0 us -> 419 us
  blocking collectives: 370 us -> 0 us
  local copies, waits for them, and re-layouts: 204 us -> 3.32 us
  other arithmetic: 92.2 us -> 0 us
  matrix products: 72.1 us -> 0 us
    pallas_call x0 -> x2, Pallas kernels: none -> 419 us  [the longest x1 391 us: spread(): pl.pallas_call(functools.partial(spread_kernel, n_inp, n_time), out_shape...]
    all_to_all x1 -> x0, blocking collectives: 370 us -> none  [on_device(): lax.all_to_all(parcel, ('inp', 'tm'), split_axis=1, concat_axis=0, tiled=...]
    reshape x2 -> x0, local copies, waits for them, and re-layouts: 114 us -> none  [the longest x1 77.6 us: correlate(): gram = gram.reshape(count, 2, inputs_all, 2, inputs_all)]
    transpose x1 -> x0, local copies, waits for them, and re-layouts: 75.4 us -> none  [correlate(): jnp.einsum('ptcraf,qtcsbf->crpasqb', blocks, blocks, preferred_element_ty...]
    dot_general x2 -> x0, matrix products: 72.1 us -> none  [the longest x1 36.1 us: correlate(): jnp.einsum('ptcraf,qtcsbf->crpasqb', blocks, blocks, preferred_element_ty...]
    convert_element_type x1 -> x0, other arithmetic: 35.4 us -> none  [on_device(): filtered = filtered.astype(jnp.bfloat16)]
    div x2 -> x0, other arithmetic: 35.2 us -> none  [the longest x1 17.6 us: correlate(): imag_part = (gram[:, 1, :, 0, :] - gram[:, 0, :, 1, :]) / frames_all]
    another operation x2 -> x0, other arithmetic: 21.6 us -> none  [the longest x1 13 us: correlate(): return jnp.stack([real_part, imag_part], axis=1)]
  transfers between devices with their start and end apart: 1 -> 1, of which waited for: 0 -> 1; matrix products, arithmetic and copies ran while one was open for 1% -> 0% of each run, Pallas kernels for 0% -> 0%
where the time goes in v1:
time: 427 us; the launch traced here: 426 us
  Pallas kernels  419 us (98%)
    pallas_call x1, Pallas kernels, spread(): pl.pallas_call(functools.partial(spread_kernel, n_inp, n_time), out_shape...  391 us
    pallas_call x1, Pallas kernels, correlate(): pl.pallas_call(functools.partial(correlate_kernel, n_inp, 1.0 / frames_al...  28.7 us
  transfers between devices with their start and end apart: 1, of which 1 were waited for; matrix products, arithmetic and copies ran while one was open for 0% of the time, Pallas kernels for 0%

profile of v1, /device:TPU:16, one launch (start us, length us, event | category | flops | bytes accessed | tf_op | source)
XLA Modules:
  0.0 426.3 jit_solution(10484041573370982314)
XLA Ops:
  0.0 2.1 slice.3
  2.1 0.3 copy.8
  2.5 1.8 collective-permute-start
  4.3 1.8 collective-permute-done.before_ref
  6.1 0.0 copy-start
  6.1 0.9 copy-done
  7.0 390.6 %filter_transform_spread.1.block_ref = bf16[32,32,64,128]{3,2,1,0:T(8,128)(2,1)} custom-call(bf16[128,64,1024]{2,1,0:T(8,128)(2,1)} %x_hbm.1, bf16[3,128,1024]{2,1,0:T(8,128)(2,1)} %copy-done, f32[512,128]{1,0:T(8,128)} %gain_ref.1, bf16[1024,1024]{1,0:T(8,128)(2,1)} %constant.4.clone.table_ref, f32[4,1024]{1,0:T(4,128)} %constant.5.clone.window_ref), custom_call_target="tpu_custom_call" | custom-call | flops 17179869184 | bytes 33554432 | tf_op jit(solution)/shard_map/filter_transform_spread/pallas_call | solution.py:239
  397.6 28.7 %correlate.1 = f32[16,2,512,512]{3,2,1,0:T(8,128)} custom-call(bf16[32,32,64,128]{3,2,1,0:T(8,128)(2,1)} %filter_transform_spread.1.block_ref), custom_call_target="tpu_custom_call" | custom-call | flops 17179869184 | bytes 50331648 | tf_op jit(solution)/shard_map/correlate/pallas_call | solution.py:297
Async XLA Ops:
  2.5 3.6 collective-permute-start
  6.1 0.9 copy-start

commit v2 on v1

--- a/solution.py
+++ b/solution.py
@@ -81,10 +81,10 @@
 
 def spread_kernel(
     n_inp, n_time,
-    x_hbm, before_ref, gain_ref, table_ref, window_ref,
+    x_hbm, gain_ref, table_ref, window_ref,
     recv_hbm,
-    xbuf, turned, taps_buf, history, filt, freq, send,
-    load_sem, send_sem, recv_sem, own_sem,
+    xbuf, turned, tail, taps_buf, halo_out, halo_in, filt, freq, send,
+    load_sem, send_sem, recv_sem, halo_send_sem, halo_recv_sem, own_sem,
 ):
     groups = n_inp * n_time
     inputs, frames, nfft = x_hbm.shape
@@ -94,17 +94,20 @@
     pitch = freq.shape[0] // STEP
     steps = frames // STEP
     tiles = nfft // LANES
+    keep = TAPS - 1
     z = lax.axis_index("inp")
     t = lax.axis_index("tm")
     me = z * n_time + t
 
-    def load(step, slot):
+    def load(step):
         f0 = pl.multiple_of(step * STEP, STEP)
+        slot = lax.rem(step, 2)
         return pltpu.make_async_copy(
             x_hbm.at[:, pl.ds(f0, STEP), :], xbuf.at[slot], load_sem.at[slot]
         )
 
-    load(0, 0).start()
+    load(steps - 1).start()
+    load(steps - 2).start()
     barrier = pltpu.get_barrier_semaphore()
 
     @pl.loop(1, groups)
@@ -115,9 +118,8 @@
             device_id_type=pl.DeviceIdType.MESH,
         )
 
-    history[...] = before_ref[...].astype(jnp.float32)
-
-    def send_one(step, d_z, d_t):
+    def send_one(step, d_z, s):
+        d_t = lax.rem(t + s, n_time)
         f0 = pl.multiple_of(step * STEP, STEP)
         d = d_z * n_time + d_t
         r0 = pl.multiple_of(d * rows_dev, rows_dev)
@@ -130,17 +132,44 @@
             device_id_type=pl.DeviceIdType.MESH,
         ).start()
 
-    def filter_step(slot):
+    def halo():
+        return pltpu.make_async_remote_copy(
+            src_ref=halo_out,
+            dst_ref=halo_in,
+            send_sem=halo_send_sem,
+            recv_sem=halo_recv_sem,
+            device_id=(z, lax.rem(t + 1, n_time)),
+            device_id_type=pl.DeviceIdType.MESH,
+        )
+
+    def filter_step(step):
+        slot = lax.rem(step, 2)
+
         @pl.loop(0, tiles)
         def _(tile):
             lanes = pl.ds(pl.multiple_of(tile * LANES, LANES), LANES)
             turned[...] = (
                 xbuf[slot, :, :, lanes].astype(jnp.float32).reshape(inputs * STEP, LANES)
             )
-            taps_buf[0 : TAPS - 1] = history[:, :, lanes]
+
+            @pl.when(step > 0)
+            def _():
+                earlier = xbuf[1 - slot, :, :, lanes].astype(jnp.float32)[:, STEP - 8 :, :]
+                tail[...] = earlier.reshape(inputs * 8, LANES)
+                for k in range(keep):
+                    taps_buf[k] = tail[pl.ds(8 - keep + k, inputs, stride=8), :]
+
+            @pl.when(step == 0)
+            def _():
+                taps_buf[0:keep] = halo_in[:, :, lanes].astype(jnp.float32)
+
             for f in range(STEP):
-                taps_buf[TAPS - 1 + f] = turned[pl.ds(f, inputs, stride=STEP), :]
-            history[:, :, lanes] = taps_buf[STEP : STEP + TAPS - 1]
+                taps_buf[keep + f] = turned[pl.ds(f, inputs, stride=STEP), :]
+
+            @pl.when(step == steps - 1)
+            def _():
+                halo_out[:, :, lanes] = taps_buf[STEP : STEP + keep].astype(jnp.bfloat16)
+
             for f in range(STEP):
                 total = window_ref[0:1, lanes] * taps_buf[f]
                 for tap in range(1, TAPS):
@@ -174,50 +203,78 @@
     far = lax.rem(z + 2, 4)
     farther = 3 - z
     near = z + 1 - 2 * lax.rem(z, 2)
+    half = n_time // 2
 
     @pl.loop(0, steps)
-    def _(step):
-        slot = lax.rem(step, 2)
-        load(step, slot).wait()
-
-        @pl.when(step + 1 < steps)
+    def _(turn):
+        step = steps - 1 - turn
+
+        @pl.when(turn == 0)
         def _():
-            load(step + 1, 1 - slot).start()
-
-        filter_step(slot)
-        transform(step, far)
+            load(steps - 1).wait()
+
+        @pl.when(step > 0)
+        def _():
+            load(step - 1).wait()
 
         @pl.when(step == 0)
         def _():
+            @pl.when(t > 0)
+            def _():
+                halo().wait_recv()
+
+            @pl.when(t == 0)
+            def _():
+                halo_in[...] = jnp.zeros_like(halo_in)
+
+        filter_step(step)
+
+        @pl.when(step > 1)
+        def _():
+            load(step - 2).start()
+
+        transform(step, far)
+
+        @pl.when(turn == 0)
+        def _():
             pl.semaphore_wait(barrier, groups - 1)
+
+            @pl.when(t < n_time - 1)
+            def _():
+                halo().start()
+
+        @pl.loop(0, half)
+        def _(s):
+            send_one(step, far, s)
+
+        transform(step, z)
+
+        @pl.loop(0, half)
+        def _(s):
+            send_one(step, far, s + half)
+            send_one(step, z, s + half)
+
+            @pl.when(s > 0)
+            def _():
+                send_one(step, z, s)
+
+        transform(step, near)
+        transform(step, farther)
 
         @pl.loop(0, n_time)
         def _(s):
-            send_one(step, far, lax.rem(t + s, n_time))
-
-            @pl.when((step > 0) & (s > 0))
-            def _():
-                send_one(step - 1, z, lax.rem(t + s, n_time))
-
-        transform(step, near)
-        transform(step, farther)
-
-        @pl.loop(0, n_time)
-        def _(s):
-            send_one(step, farther, lax.rem(t + s, n_time))
-            send_one(step, near, lax.rem(t + s, n_time))
-
-        transform(step, z)
-
-    @pl.loop(1, n_time)
-    def _(s):
-        send_one(steps - 1, z, lax.rem(t + s, n_time))
+            send_one(step, near, s)
+            send_one(step, farther, s)
 
     own = pltpu.make_async_copy(
         send.at[pl.ds(pl.multiple_of(me * rows_dev, rows_dev), rows_dev)], recv_hbm.at[me], own_sem
     )
     own.start()
     own.wait()
+
+    @pl.when(t < n_time - 1)
+    def _():
+        halo().wait_send()
 
     @pl.loop(1, groups)
     def _(s):
@@ -228,7 +285,7 @@
         pltpu.make_async_copy(here, here, recv_sem.at[d]).wait()
 
 
-def spread(samples, before, eq_gain, n_inp, n_time):
+def spread(samples, eq_gain, n_inp, n_time):
     inputs, frames, nfft = samples.shape
     channels = nfft // 2
     rows = 2 * channels
@@ -239,19 +296,23 @@
     return pl.pallas_call(
         functools.partial(spread_kernel, n_inp, n_time),
         out_shape=jax.ShapeDtypeStruct((groups, rows // groups, frames, inputs), jnp.bfloat16),
-        in_specs=[anywhere, vmem, vmem, vmem, vmem],
+        in_specs=[anywhere, vmem, vmem, vmem],
         out_specs=anywhere,
         scratch_shapes=[
             pltpu.VMEM((2, inputs, STEP, nfft), jnp.bfloat16),
             pltpu.VMEM((inputs * STEP, LANES), jnp.float32),
+            pltpu.VMEM((inputs * 8, LANES), jnp.float32),
             pltpu.VMEM((STEP + TAPS - 1, inputs, LANES), jnp.float32),
-            pltpu.VMEM((TAPS - 1, inputs, nfft), jnp.float32),
+            pltpu.VMEM((TAPS - 1, inputs, nfft), jnp.bfloat16),
+            pltpu.VMEM((TAPS - 1, inputs, nfft), jnp.bfloat16),
             pltpu.VMEM((STEP * inputs, nfft), jnp.bfloat16),
             pltpu.VMEM((STEP * pitch, LANES), jnp.float32),
             pltpu.VMEM((rows, frames, inputs), jnp.bfloat16),
             pltpu.SemaphoreType.DMA((2,)),
             pltpu.SemaphoreType.DMA((groups,)),
             pltpu.SemaphoreType.DMA((groups,)),
+            pltpu.SemaphoreType.DMA,
+            pltpu.SemaphoreType.DMA,
             pltpu.SemaphoreType.DMA,
         ],
         compiler_params=pltpu.CompilerParams(
@@ -264,29 +325,40 @@
         ),
         name="filter_transform_spread",
     )(
-        samples, before, eq_gain,
+        samples, eq_gain,
         jnp.asarray(fourier_table(channels, nfft)), jnp.asarray(window_table(TAPS, nfft)),
     )
 
 
 def correlate_kernel(n_inp, scale, block_ref, out_ref):
-    sources, _, frames, inputs = block_ref.shape
+    sources, rows, frames, inputs = block_ref.shape
     n_time = sources // n_inp
-
-    def part(r):
+    half = n_inp * inputs // 2
+
+    def part(row):
         pieces = [
-            block_ref[p * n_time : (p + 1) * n_time, r].reshape(n_time * frames, inputs)
+            block_ref[p * n_time : (p + 1) * n_time, row].reshape(n_time * frames, inputs)
             for p in range(n_inp)
         ]
         return jnp.concatenate(pieces, axis=1)
 
-    real, imag = part(0), part(1)
-    real_t, imag_t = real.T, imag.T
-    right = jnp.concatenate([real, imag], axis=0)
-    left = jnp.concatenate([real_t, imag_t], axis=1)
-    out_ref[0, 0] = jnp.dot(left, right, preferred_element_type=jnp.float32) * scale
-    left = jnp.concatenate([imag_t, -real_t], axis=1)
-    out_ref[0, 1] = jnp.dot(left, right, preferred_element_type=jnp.float32) * scale
+    for chan in range(rows // 2):
+        real, imag = part(2 * chan), part(2 * chan + 1)
+        real_t, imag_t = real.T, imag.T
+        right = jnp.concatenate([real, imag], axis=0)
+        for kind, left in enumerate(
+            [
+                jnp.concatenate([real_t, imag_t], axis=1),
+                jnp.concatenate([imag_t, -real_t], axis=1),
+            ]
+        ):
+            upper = jnp.dot(left[:half], right, preferred_element_type=jnp.float32) * scale
+            corner = upper[:, half:].T
+            out_ref[chan, kind, 0:half, :] = upper
+            out_ref[chan, kind, half:, 0:half] = -corner if kind else corner
+            out_ref[chan, kind, half:, half:] = (
+                jnp.dot(left[half:], right[:, half:], preferred_element_type=jnp.float32) * scale
+            )
 
 
 def correlate(arrived, n_inp):
@@ -296,10 +368,10 @@
     frames_all = sources // n_inp * frames
     return pl.pallas_call(
         functools.partial(correlate_kernel, n_inp, 1.0 / frames_all),
-        grid=(count,),
+        grid=(count // 2,),
         out_shape=jax.ShapeDtypeStruct((count, 2, inputs_all, inputs_all), jnp.float32),
-        in_specs=[pl.BlockSpec((sources, 2, frames, inputs), lambda c: (0, c, 0, 0))],
-        out_specs=pl.BlockSpec((1, 2, inputs_all, inputs_all), lambda c: (c, 0, 0, 0)),
+        in_specs=[pl.BlockSpec((sources, 4, frames, inputs), lambda c: (0, c, 0, 0))],
+        out_specs=pl.BlockSpec((2, 2, inputs_all, inputs_all), lambda c: (c, 0, 0, 0)),
         compiler_params=pltpu.CompilerParams(vmem_limit_bytes=48 * 1024 * 1024),
         cost_estimate=pl.CostEstimate(
             flops=count * 8 * inputs_all * inputs_all * frames_all,
@@ -314,11 +386,9 @@
     local_inputs, local_frames, nfft = samples.shape
     n_inp = lax.axis_size("inp")
     n_time = lax.axis_size("tm")
-    if local_inputs != LANES or n_inp != 4 or n_time != 8 or local_frames % STEP:
+    if local_inputs != LANES or n_inp != 4 or n_time != 8 or local_frames % STEP or local_frames < 2 * STEP:
         return plain_plan(samples, eq_gain)
-    tail = jnp.swapaxes(samples[:, local_frames - (TAPS - 1) :, :], 0, 1)
-    before = passed_along(tail, "tm", 1)
-    arrived = spread(samples, before, eq_gain, n_inp, n_time)
+    arrived = spread(samples, eq_gain, n_inp, n_time)
     return correlate(arrived, n_inp)
 
 

time: 427 us -> 408 us (0.956)
  Pallas kernels: 419 us -> 408 us
    pallas_call x1, Pallas kernels: 391 us -> 385 us  [spread(): pl.pallas_call(functools.partial(spread_kernel, n_inp, n_time), out_shape...]
    pallas_call x1, Pallas kernels: 28.7 us -> 23 us  [correlate(): pl.pallas_call(functools.partial(correlate_kernel, n_inp, 1.0 / frames_al...]
  transfers between devices with their start and end apart: 1 -> 0, of which waited for: 1 -> 0; matrix products, arithmetic and copies ran while one was open for 0% -> 0% of each run, Pallas kernels for 0% -> 0%
where the time goes in v2:
time: 408 us
  Pallas kernels  408 us (100%)
    pallas_call x1, Pallas kernels, spread(): pl.pallas_call(functools.partial(spread_kernel, n_inp, n_time), out_shape...  385 us
    pallas_call x1, Pallas kernels, correlate(): pl.pallas_call(functools.partial(correlate_kernel, n_inp, 1.0 / frames_al...  23 us

profile of v2, /device:TPU:16, one launch (start us, length us, event | category | flops | bytes accessed | tf_op | source)
XLA Modules:
  0.0 407.6 jit_solution(12144733452123654682)
XLA Ops:
  0.0 384.5 %filter_transform_spread.1.block_ref = bf16[32,32,64,128]{3,2,1,0:T(8,128)(2,1)} custom-call(bf16[128,64,1024]{2,1,0:T(8,128)(2,1)} %x_hbm.1, f32[512,128]{1,0:T(8,128)} %gain_ref.1, bf16[1024,1024]{1,0:T(8,128)(2,1)} %constant.4.clone.table_ref, f32[4,1024]{1,0:T(4,128)} %constant.5.clone.window_ref), custom_call_target="tpu_custom_call" | custom-call | flops 17179869184 | bytes 33554432 | tf_op jit(solution)/shard_map/filter_transform_spread/pallas_call | solution.py:296
  384.5 23.0 %correlate.1 = f32[16,2,512,512]{3,2,1,0:T(8,128)} custom-call(bf16[32,32,64,128]{3,2,1,0:T(8,128)(2,1)} %filter_transform_spread.1.block_ref), custom_call_target="tpu_custom_call" | custom-call | flops 17179869184 | bytes 50331648 | tf_op jit(solution)/shard_map/correlate/pallas_call | solution.py:369

commit v3 on v2

--- a/solution.py
+++ b/solution.py
@@ -82,9 +82,9 @@
 def spread_kernel(
     n_inp, n_time,
     x_hbm, gain_ref, table_ref, window_ref,
-    recv_hbm,
+    recv_hbm, late_hbm,
     xbuf, turned, tail, taps_buf, halo_out, halo_in, filt, freq, send,
-    load_sem, send_sem, recv_sem, halo_send_sem, halo_recv_sem, own_sem,
+    load_sem, send_sem, recv_sem, halo_send_sem, halo_recv_sem, own_sem, late_sem,
 ):
     groups = n_inp * n_time
     inputs, frames, nfft = x_hbm.shape
@@ -118,14 +118,16 @@
             device_id_type=pl.DeviceIdType.MESH,
         )
 
-    def send_one(step, d_z, s):
+    rows_first = rows_dev // 2
+
+    def send_one(step, d_z, s, count=rows_dev):
         d_t = lax.rem(t + s, n_time)
         f0 = pl.multiple_of(step * STEP, STEP)
         d = d_z * n_time + d_t
         r0 = pl.multiple_of(d * rows_dev, rows_dev)
         pltpu.make_async_remote_copy(
-            src_ref=send.at[pl.ds(r0, rows_dev), pl.ds(f0, STEP), :],
-            dst_ref=recv_hbm.at[me, :, pl.ds(f0, STEP), :],
+            src_ref=send.at[pl.ds(r0, count), pl.ds(f0, STEP), :],
+            dst_ref=recv_hbm.at[me, pl.ds(0, count), pl.ds(f0, STEP), :],
             send_sem=send_sem.at[d],
             recv_sem=recv_sem.at[me],
             device_id=(d_z, d_t),
@@ -243,7 +245,9 @@
             def _():
                 halo().start()
 
-        @pl.loop(0, half)
+        send_one(step, far, 0, rows_first)
+
+        @pl.loop(1, half)
         def _(s):
             send_one(step, far, s)
 
@@ -270,19 +274,34 @@
         send.at[pl.ds(pl.multiple_of(me * rows_dev, rows_dev), rows_dev)], recv_hbm.at[me], own_sem
     )
     own.start()
+    partner = far * n_time + t
+    late_row = pl.multiple_of(partner * rows_dev + rows_first, rows_first)
+    late = pltpu.make_async_copy(send.at[pl.ds(late_row, rows_first)], late_hbm, late_sem)
+    late.start()
     own.wait()
+    late.wait()
 
     @pl.when(t < n_time - 1)
     def _():
         halo().wait_send()
 
+    def finish(d, count):
+        gone = send.at[pl.ds(pl.multiple_of(d * rows_dev, rows_dev), count)]
+        pltpu.make_async_copy(gone, gone, send_sem.at[d]).wait()
+        here = recv_hbm.at[d, pl.ds(0, count)]
+        pltpu.make_async_copy(here, here, recv_sem.at[d]).wait()
+
     @pl.loop(1, groups)
     def _(s):
         d = lax.rem(me + s, groups)
-        gone = send.at[pl.ds(pl.multiple_of(d * rows_dev, rows_dev), rows_dev)]
-        pltpu.make_async_copy(gone, gone, send_sem.at[d]).wait()
-        here = recv_hbm.at[d]
-        pltpu.make_async_copy(here, here, recv_sem.at[d]).wait()
+
+        @pl.when(d == partner)
+        def _():
+            finish(d, rows_first)
+
+        @pl.when(d != partner)
+        def _():
+            finish(d, rows_dev)
 
 
 def spread(samples, eq_gain, n_inp, n_time):
@@ -295,9 +314,12 @@
     anywhere = pl.BlockSpec(memory_space=pl.ANY)
     return pl.pallas_call(
         functools.partial(spread_kernel, n_inp, n_time),
-        out_shape=jax.ShapeDtypeStruct((groups, rows // groups, frames, inputs), jnp.bfloat16),
+        out_shape=[
+            jax.ShapeDtypeStruct((groups, rows // groups, frames, inputs), jnp.bfloat16),
+            jax.ShapeDtypeStruct((rows // groups // 2, frames, inputs), jnp.bfloat16),
+        ],
         in_specs=[anywhere, vmem, vmem, vmem],
-        out_specs=anywhere,
+        out_specs=[anywhere, anywhere],
         scratch_shapes=[
             pltpu.VMEM((2, inputs, STEP, nfft), jnp.bfloat16),
             pltpu.VMEM((inputs * STEP, LANES), jnp.float32),
@@ -311,6 +333,7 @@
             pltpu.SemaphoreType.DMA((2,)),
             pltpu.SemaphoreType.DMA((groups,)),
             pltpu.SemaphoreType.DMA((groups,)),
+            pltpu.SemaphoreType.DMA,
             pltpu.SemaphoreType.DMA,
             pltpu.SemaphoreType.DMA,
             pltpu.SemaphoreType.DMA,
@@ -330,14 +353,23 @@
     )
 
 
-def correlate_kernel(n_inp, scale, block_ref, out_ref):
+def correlate_kernel(n_inp, scale, block_ref, *refs):
+    late_ref = refs[0] if len(refs) > 1 else None
+    out_ref = refs[-1]
     sources, rows, frames, inputs = block_ref.shape
     n_time = sources // n_inp
     half = n_inp * inputs // 2
+    if late_ref is not None:
+        partner = lax.rem(lax.axis_index("inp") + 2, 4) * n_time + lax.axis_index("tm")
+
+    def from_source(src, row):
+        if late_ref is None:
+            return block_ref[src, row]
+        return jnp.where(partner == src, late_ref[row], block_ref[src, row])
 
     def part(row):
         pieces = [
-            block_ref[p * n_time : (p + 1) * n_time, row].reshape(n_time * frames, inputs)
+            jnp.concatenate([from_source(p * n_time + q, row) for q in range(n_time)], axis=0)
             for p in range(n_inp)
         ]
         return jnp.concatenate(pieces, axis=1)
@@ -361,25 +393,39 @@
             )
 
 
-def correlate(arrived, n_inp):
+def correlate(arrived, n_inp, late=None, before=None):
     sources, rows, frames, inputs = arrived.shape
     count = rows // 2
     inputs_all = n_inp * inputs
     frames_all = sources // n_inp * frames
+    turns = count // 4
+    first = 0 if before is None else turns
+    in_specs = [pl.BlockSpec((sources, 4, frames, inputs), lambda c: (0, c + first, 0, 0))]
+    operands = [arrived]
+    aliases = {}
+    body = functools.partial(correlate_kernel, n_inp, 1.0 / frames_all)
+    if before is not None:
+        in_specs.append(pl.BlockSpec((4, frames, inputs), lambda c: (c, 0, 0)))
+        in_specs.append(pl.BlockSpec(memory_space=pl.ANY))
+        operands += [late, before]
+        aliases = {2: 0}
+        whole = body
+        body = lambda block_ref, late_ref, _, out_ref: whole(block_ref, late_ref, out_ref)
     return pl.pallas_call(
-        functools.partial(correlate_kernel, n_inp, 1.0 / frames_all),
-        grid=(count // 2,),
+        body,
+        grid=(turns,),
         out_shape=jax.ShapeDtypeStruct((count, 2, inputs_all, inputs_all), jnp.float32),
-        in_specs=[pl.BlockSpec((sources, 4, frames, inputs), lambda c: (0, c, 0, 0))],
-        out_specs=pl.BlockSpec((2, 2, inputs_all, inputs_all), lambda c: (c, 0, 0, 0)),
+        in_specs=in_specs,
+        out_specs=pl.BlockSpec((2, 2, inputs_all, inputs_all), lambda c: (c + first, 0, 0, 0)),
+        input_output_aliases=aliases,
         compiler_params=pltpu.CompilerParams(vmem_limit_bytes=48 * 1024 * 1024),
         cost_estimate=pl.CostEstimate(
-            flops=count * 8 * inputs_all * inputs_all * frames_all,
-            bytes_accessed=arrived.size * 2 + count * 8 * inputs_all * inputs_all,
+            flops=count * 3 * inputs_all * inputs_all * frames_all,
+            bytes_accessed=arrived.size + count * 4 * inputs_all * inputs_all,
             transcendentals=0,
         ),
-        name="correlate",
-    )(arrived)
+        name="correlate_first" if before is None else "correlate_second",
+    )(*operands)
 
 
 def on_device(samples, eq_gain):
@@ -388,8 +434,10 @@
     n_time = lax.axis_size("tm")
     if local_inputs != LANES or n_inp != 4 or n_time != 8 or local_frames % STEP or local_frames < 2 * STEP:
         return plain_plan(samples, eq_gain)
-    arrived = spread(samples, eq_gain, n_inp, n_time)
-    return correlate(arrived, n_inp)
+    arrived, late = spread(samples, eq_gain, n_inp, n_time)
+    late = lax.ppermute(late, "inp", [(i, (i + 2) % n_inp) for i in range(n_inp)])
+    first = correlate(arrived, n_inp)
+    return correlate(arrived, n_inp, late, first)
 
 
 def solution(mesh):

time: 408 us -> 403 us (0.988)
  Pallas kernels: 408 us -> 399 us
    pallas_call x1, Pallas kernels: 385 us -> 373 us  [spread(): pl.pallas_call(functools.partial(spread_kernel, n_inp, n_time), out_shape...]
    pallas_call x1 -> x2, Pallas kernels: 23 us -> 25.4 us  [correlate(): pl.pallas_call(body, grid=(turns,), out_shape=jax.ShapeDtypeStruct((count...]
  transfers between devices with their start and end apart: 0 -> 1, of which waited for: 0 -> 0; matrix products, arithmetic and copies ran while one was open for 0% -> 0% of each run, Pallas kernels for 0% -> 3%
where the time goes in v3:
time: 403 us; the launch traced here: 399 us
  Pallas kernels  399 us (99%)
    pallas_call x1, Pallas kernels, spread(): pl.pallas_call(functools.partial(spread_kernel, n_inp, n_time), out_shape...  373 us
    pallas_call x2, Pallas kernels, correlate(): pl.pallas_call(body, grid=(turns,), out_shape=jax.ShapeDtypeStruct((count...  25.4 us
  transfers between devices with their start and end apart: 1, of which 0 were waited for; matrix products, arithmetic and copies ran while one was open for 0% of the time, Pallas kernels for 3%

profile of v3, /device:TPU:16, one launch (start us, length us, event | category | flops | bytes accessed | tf_op | source)
XLA Modules:
  0.0 398.9 jit_solution(4741315032641964406)
XLA Ops:
  0.0 373.4 %filter_transform_spread.1 = (bf16[32,32,64,128]{3,2,1,0:T(8,128)(2,1)}, bf16[16,64,128]{2,1,0:T(8,128)(2,1)}) custom-call(bf16[128,64,1024]{2,1,0:T(8,128)(2,1)} %x_hbm.1, f32[512,128]{1,0:T(8,128)} %gain_ref.1, bf16[1024,1024]{1,0:T(8,128)(2,1)} %constant.4.clone.table_ref, f32[4,1024]{1,0:T(4,128)} %constant.5.clone.window_ref), custom_call_target="tpu_custom_call" | custom-call | flops 17179869184 | bytes 33554432 | tf_op jit(solution)/shard_map/filter_transform_spread/pallas_call | solution.py:315
  373.4 0.1 collective-permute-start
  373.5 12.7 %correlate_first.1._ = f32[16,2,512,512]{3,2,1,0:T(8,128)} custom-call(bf16[32,32,64,128]{3,2,1,0:T(8,128)(2,1)} %get-tuple-element.7.block_ref), custom_call_target="tpu_custom_call" | custom-call | flops 6442450944 | bytes 25165824 | tf_op jit(solution)/shard_map/correlate_first/pallas_call | solution.py:414
  386.2 0.0 collective-permute-done.late_ref
  386.2 12.7 %correlate_second.1 = f32[16,2,512,512]{3,2,1,0:T(8,128)} custom-call(bf16[32,32,64,128]{3,2,1,0:T(8,128)(2,1)} %get-tuple-element.7.block_ref, bf16[16,64,128]{2,1,0:T(8,128)(2,1)S(1)} %collective-permute-done.late_ref, f32[16,2,512,512]{3,2,1,0:T(8,128)} %correlate_first.1._), custom_call_target="tpu_custom_call", output_to_operand_aliasing={{}: (2, {})} | custom-call | flops 6442450944 | bytes 25165824 | tf_op jit(solution)/shard_map/correlate_second/pallas_call | solution.py:414
Async XLA Ops:
  373.4 12.8 %collective-permute-start = (bf16[16,64,128]{2,1,0:T(8,128)(2,1)}, bf16[16,64,128]{2,1,0:T(8,128)(2,1)S(1)}, u32[]{:S(2)}, u32[]{:S(2)}) collective-permute-start(bf16[16,64,128]{2,1,0:T(8,128)(2,1)} %get-tuple-element.8), channel_id=1, source_target_pairs={{0,16},{8,24},{16,0},{24,8},{1,17},{9,25},{17,1},{25,9},{2,18},{10... | collective-permute-start | bytes 786440 | tf_op jit(solution)/shard_map/ppermute | solution.py:438

commit v4 on v3

--- a/solution.py
+++ b/solution.py
@@ -82,7 +82,7 @@
 def spread_kernel(
     n_inp, n_time,
     x_hbm, gain_ref, table_ref, window_ref,
-    recv_hbm, late_hbm,
+    recv_hbm, late_far_hbm, late_farther_hbm,
     xbuf, turned, tail, taps_buf, halo_out, halo_in, filt, freq, send,
     load_sem, send_sem, recv_sem, halo_send_sem, halo_recv_sem, own_sem, late_sem,
 ):
@@ -118,7 +118,8 @@
             device_id_type=pl.DeviceIdType.MESH,
         )
 
-    rows_first = rows_dev // 2
+    rows_late = late_far_hbm.shape[0]
+    rows_first = rows_dev - rows_late
 
     def send_one(step, d_z, s, count=rows_dev):
         d_t = lax.rem(t + s, n_time)
@@ -163,20 +164,30 @@
 
             @pl.when(step == 0)
             def _():
-                taps_buf[0:keep] = halo_in[:, :, lanes].astype(jnp.float32)
-
-            for f in range(STEP):
-                taps_buf[keep + f] = turned[pl.ds(f, inputs, stride=STEP), :]
+                taps_buf[...] = halo_in[:, :, lanes].astype(jnp.float32)
 
             @pl.when(step == steps - 1)
             def _():
-                halo_out[:, :, lanes] = taps_buf[STEP : STEP + keep].astype(jnp.bfloat16)
-
-            for f in range(STEP):
-                total = window_ref[0:1, lanes] * taps_buf[f]
-                for tap in range(1, TAPS):
-                    total = total + window_ref[tap : tap + 1, lanes] * taps_buf[f + tap]
-                filt[f * inputs : (f + 1) * inputs, lanes] = total.astype(jnp.bfloat16)
+                for k in range(keep):
+                    last = turned[pl.ds(STEP - keep + k, inputs, stride=STEP), :]
+                    halo_out[k, :, lanes] = last.astype(jnp.bfloat16)
+
+            some = 32
+            weights = [
+                jnp.broadcast_to(window_ref[tap : tap + 1, lanes], (some, LANES))
+                for tap in range(TAPS)
+            ]
+            for i0 in range(0, inputs, some):
+                held = [taps_buf[k, i0 : i0 + some] for k in range(keep)]
+                for f in range(STEP):
+                    held.append(turned[pl.ds(i0 * STEP + f, some, stride=STEP), :])
+                    total = weights[0] * held[0]
+                    for tap in range(1, TAPS):
+                        total = total + weights[tap] * held[tap]
+                    filt[f * inputs + i0 : f * inputs + i0 + some, lanes] = total.astype(
+                        jnp.bfloat16
+                    )
+                    held.pop(0)
 
     def transform(step, plane):
         f0 = pl.multiple_of(step * STEP, STEP)
@@ -265,7 +276,10 @@
         transform(step, near)
         transform(step, farther)
 
-        @pl.loop(0, n_time)
+        send_one(step, near, 0)
+        send_one(step, farther, 0, rows_first)
+
+        @pl.loop(1, n_time)
         def _(s):
             send_one(step, near, s)
             send_one(step, farther, s)
@@ -274,12 +288,18 @@
         send.at[pl.ds(pl.multiple_of(me * rows_dev, rows_dev), rows_dev)], recv_hbm.at[me], own_sem
     )
     own.start()
-    partner = far * n_time + t
-    late_row = pl.multiple_of(partner * rows_dev + rows_first, rows_first)
-    late = pltpu.make_async_copy(send.at[pl.ds(late_row, rows_first)], late_hbm, late_sem)
-    late.start()
+    partners = (far * n_time + t, farther * n_time + t)
+    late = [
+        pltpu.make_async_copy(
+            send.at[pl.ds(partner * rows_dev + rows_first, rows_late)], late_hbm, late_sem.at[k]
+        )
+        for k, (partner, late_hbm) in enumerate(zip(partners, (late_far_hbm, late_farther_hbm)))
+    ]
+    for copy in late:
+        copy.start()
     own.wait()
-    late.wait()
+    for copy in late:
+        copy.wait()
 
     @pl.when(t < n_time - 1)
     def _():
@@ -295,16 +315,16 @@
     def _(s):
         d = lax.rem(me + s, groups)
 
-        @pl.when(d == partner)
+        @pl.when((d == partners[0]) | (d == partners[1]))
         def _():
             finish(d, rows_first)
 
-        @pl.when(d != partner)
+        @pl.when((d != partners[0]) & (d != partners[1]))
         def _():
             finish(d, rows_dev)
 
 
-def spread(samples, eq_gain, n_inp, n_time):
+def spread(samples, eq_gain, n_inp, n_time, late):
     inputs, frames, nfft = samples.shape
     channels = nfft // 2
     rows = 2 * channels
@@ -316,15 +336,16 @@
         functools.partial(spread_kernel, n_inp, n_time),
         out_shape=[
             jax.ShapeDtypeStruct((groups, rows // groups, frames, inputs), jnp.bfloat16),
-            jax.ShapeDtypeStruct((rows // groups // 2, frames, inputs), jnp.bfloat16),
+            jax.ShapeDtypeStruct((2 * late, frames, inputs), jnp.bfloat16),
+            jax.ShapeDtypeStruct((2 * late, frames, inputs), jnp.bfloat16),
         ],
         in_specs=[anywhere, vmem, vmem, vmem],
-        out_specs=[anywhere, anywhere],
+        out_specs=[anywhere] * 3,
         scratch_shapes=[
             pltpu.VMEM((2, inputs, STEP, nfft), jnp.bfloat16),
             pltpu.VMEM((inputs * STEP, LANES), jnp.float32),
             pltpu.VMEM((inputs * 8, LANES), jnp.float32),
-            pltpu.VMEM((STEP + TAPS - 1, inputs, LANES), jnp.float32),
+            pltpu.VMEM((TAPS - 1, inputs, LANES), jnp.float32),
             pltpu.VMEM((TAPS - 1, inputs, nfft), jnp.bfloat16),
             pltpu.VMEM((TAPS - 1, inputs, nfft), jnp.bfloat16),
             pltpu.VMEM((STEP * inputs, nfft), jnp.bfloat16),
@@ -336,7 +357,7 @@
             pltpu.SemaphoreType.DMA,
             pltpu.SemaphoreType.DMA,
             pltpu.SemaphoreType.DMA,
-            pltpu.SemaphoreType.DMA,
+            pltpu.SemaphoreType.DMA((2,)),
         ],
         compiler_params=pltpu.CompilerParams(
             collective_id=0, has_side_effects=True, vmem_limit_bytes=56 * 1024 * 1024
@@ -354,18 +375,21 @@
 
 
 def correlate_kernel(n_inp, scale, block_ref, *refs):
-    late_ref = refs[0] if len(refs) > 1 else None
+    late_refs = refs[:-1]
     out_ref = refs[-1]
     sources, rows, frames, inputs = block_ref.shape
     n_time = sources // n_inp
     half = n_inp * inputs // 2
-    if late_ref is not None:
-        partner = lax.rem(lax.axis_index("inp") + 2, 4) * n_time + lax.axis_index("tm")
+    if late_refs:
+        z, t = lax.axis_index("inp"), lax.axis_index("tm")
+        partners = (lax.rem(z + 2, 4) * n_time + t, (3 - z) * n_time + t)
 
     def from_source(src, row):
-        if late_ref is None:
-            return block_ref[src, row]
-        return jnp.where(partner == src, late_ref[row], block_ref[src, row])
+        value = block_ref[src, row]
+        if late_refs:
+            for partner, late_ref in zip(partners, late_refs):
+                value = jnp.where(partner == src, late_ref[row], value)
+        return value
 
     def part(row):
         pieces = [
@@ -393,24 +417,24 @@
             )
 
 
-def correlate(arrived, n_inp, late=None, before=None):
+def correlate(arrived, n_inp, late_chans, late=(), before=None):
     sources, rows, frames, inputs = arrived.shape
     count = rows // 2
     inputs_all = n_inp * inputs
     frames_all = sources // n_inp * frames
-    turns = count // 4
-    first = 0 if before is None else turns
+    turns = (count - late_chans if before is None else late_chans) // 2
+    first = 0 if before is None else (count - late_chans) // 2
     in_specs = [pl.BlockSpec((sources, 4, frames, inputs), lambda c: (0, c + first, 0, 0))]
     operands = [arrived]
     aliases = {}
     body = functools.partial(correlate_kernel, n_inp, 1.0 / frames_all)
     if before is not None:
-        in_specs.append(pl.BlockSpec((4, frames, inputs), lambda c: (c, 0, 0)))
+        in_specs += [pl.BlockSpec((4, frames, inputs), lambda c: (c, 0, 0)) for _ in late]
         in_specs.append(pl.BlockSpec(memory_space=pl.ANY))
-        operands += [late, before]
-        aliases = {2: 0}
+        operands += [*late, before]
+        aliases = {len(operands) - 1: 0}
         whole = body
-        body = lambda block_ref, late_ref, _, out_ref: whole(block_ref, late_ref, out_ref)
+        body = lambda *refs: whole(*refs[:-2], refs[-1])
     return pl.pallas_call(
         body,
         grid=(turns,),
@@ -420,8 +444,8 @@
         input_output_aliases=aliases,
         compiler_params=pltpu.CompilerParams(vmem_limit_bytes=48 * 1024 * 1024),
         cost_estimate=pl.CostEstimate(
-            flops=count * 3 * inputs_all * inputs_all * frames_all,
-            bytes_accessed=arrived.size + count * 4 * inputs_all * inputs_all,
+            flops=turns * 12 * inputs_all * inputs_all * frames_all,
+            bytes_accessed=turns * (4 * arrived.size // count + 16 * inputs_all * inputs_all),
             transcendentals=0,
         ),
         name="correlate_first" if before is None else "correlate_second",
@@ -432,12 +456,14 @@
     local_inputs, local_frames, nfft = samples.shape
     n_inp = lax.axis_size("inp")
     n_time = lax.axis_size("tm")
-    if local_inputs != LANES or n_inp != 4 or n_time != 8 or local_frames % STEP or local_frames < 2 * STEP:
+    if local_inputs != LANES or n_inp != 4 or n_time != 8 or local_frames % STEP or local_frames < 2 * STEP or nfft != 1024:
         return plain_plan(samples, eq_gain)
-    arrived, late = spread(samples, eq_gain, n_inp, n_time)
-    late = lax.ppermute(late, "inp", [(i, (i + 2) % n_inp) for i in range(n_inp)])
-    first = correlate(arrived, n_inp)
-    return correlate(arrived, n_inp, late, first)
+    late_chans = nfft // 2 // (n_inp * n_time) * 3 // 8
+    arrived, far, farther = spread(samples, eq_gain, n_inp, n_time, late_chans)
+    far = lax.ppermute(far, "inp", [(i, (i + 2) % n_inp) for i in range(n_inp)])
+    farther = lax.ppermute(farther, "inp", [(i, n_inp - 1 - i) for i in range(n_inp)])
+    first = correlate(arrived, n_inp, late_chans)
+    return correlate(arrived, n_inp, late_chans, (far, farther), first)
 
 
 def solution(mesh):

time: 403 us -> 398 us (0.988)
  Pallas kernels: 399 us -> 393 us
    pallas_call x1, Pallas kernels: 373 us -> 366 us  [spread(): pl.pallas_call(functools.partial(spread_kernel, n_inp, n_time), out_shape...]
  transfers between devices with their start and end apart: 1 -> 2, of which waited for: 0 -> 1; matrix products, arithmetic and copies ran while one was open for 0% -> 0% of each run, Pallas kernels for 3% -> 4%
where the time goes in v4:
time: 398 us; the launch traced here: 395 us
  Pallas kernels  393 us (99%)
    pallas_call x1, Pallas kernels, spread(): pl.pallas_call(functools.partial(spread_kernel, n_inp, n_time), out_shape...  366 us
    pallas_call x2, Pallas kernels, correlate(): pl.pallas_call(body, grid=(turns,), out_shape=jax.ShapeDtypeStruct((count...  26.4 us
  transfers between devices with their start and end apart: 2, of which 1 were waited for; matrix products, arithmetic and copies ran while one was open for 0% of the time, Pallas kernels for 4%

profile of v4, /device:TPU:16, one launch (start us, length us, event | category | flops | bytes accessed | tf_op | source)
XLA Modules:
  0.0 394.8 jit_solution(4051914148824500257)
XLA Ops:
  0.0 366.3 %filter_transform_spread.1 = (bf16[32,32,64,128]{3,2,1,0:T(8,128)(2,1)}, bf16[12,64,128]{2,1,0:T(8,128)(2,1)}, bf16[12,64,128]{2,1,0:T(8,128)(2,1)}) custom-call(bf16[128,64,1024]{2,1,0:T(8,128)(2,1)} %x_hbm.1, f32[512,128]{1,0:T(8,128)} %gain_ref.1, bf16[1024,1024]{1,0:T(8,128)(2,1)} %constant.4.clone.table_ref, f32[4,1024]{1,0:T(4,128)} %constant.5.clone.window_ref), custom_call_target="tpu_custom_call" | custom-call | flops 17179869184 | bytes 33554432 | tf_op jit(solution)/shard_map/filter_transform_spread/pallas_call | solution.py:335
  366.3 0.1 collective-permute-start
  366.4 0.1 collective-permute-start.1
  366.4 15.7 %correlate_first.1.refs_3_ = f32[16,2,512,512]{3,2,1,0:T(8,128)} custom-call(bf16[32,32,64,128]{3,2,1,0:T(8,128)(2,1)} %get-tuple-element.8.block_ref.refs_0_), custom_call_target="tpu_custom_call" | custom-call | flops 8053063680 | bytes 31457280 | tf_op jit(solution)/shard_map/correlate_first/pallas_call | solution.py:438
  382.2 0.0 collective-permute-done.refs_1_
  382.2 2.0 collective-permute-done.1.refs_2_
  384.1 10.7 %correlate_second.1 = f32[16,2,512,512]{3,2,1,0:T(8,128)} custom-call(bf16[32,32,64,128]{3,2,1,0:T(8,128)(2,1)} %get-tuple-element.8.block_ref.refs_0_, bf16[12,64,128]{2,1,0:T(8,128)(2,1)S(1)} %collective-permute-done.refs_1_, bf16[12,64,128]{2,1,0:T(8,128)(2,1)S(1)} %collective-permute-done.1.refs_2_, ...), custom_call_target="tpu_custom_call", output_to_operand_aliasing={{}: (3, {})} | custom-call | flops 4831838208 | bytes 18874368 | tf_op jit(solution)/shard_map/correlate_second/pallas_call | solution.py:438
Async XLA Ops:
  366.3 15.9 %collective-permute-start = (bf16[12,64,128]{2,1,0:T(8,128)(2,1)}, bf16[12,64,128]{2,1,0:T(8,128)(2,1)S(1)}, u32[]{:S(2)}, u32[]{:S(2)}) collective-permute-start(bf16[12,64,128]{2,1,0:T(8,128)(2,1)} %get-tuple-element.9), channel_id=1, source_target_pairs={{0,16},{8,24},{16,0},{24,8},{1,17},{9,25},{17,1},{25,9},{2,18},{10... | collective-permute-start | bytes 589832 | tf_op jit(solution)/shard_map/ppermute | solution.py:463
  366.4 17.8 %collective-permute-start.1 = (bf16[12,64,128]{2,1,0:T(8,128)(2,1)}, bf16[12,64,128]{2,1,0:T(8,128)(2,1)S(1)}, u32[]{:S(2)}, u32[]{:S(2)}) collective-permute-start(bf16[12,64,128]{2,1,0:T(8,128)(2,1)} %get-tuple-element.10), channel_id=1, source_target_pairs={{0,24},{8,16},{16,8},{24,0},{1,25},{9,17},{17,9},{25,1},{2,26},{10... | collective-permute-start | bytes 589832 | tf_op jit(solution)/shard_map/ppermute | solution.py:464

commit v5 on v4

--- a/solution.py
+++ b/solution.py
@@ -398,23 +398,29 @@
         ]
         return jnp.concatenate(pieces, axis=1)
 
+    chans = []
     for chan in range(rows // 2):
         real, imag = part(2 * chan), part(2 * chan + 1)
-        real_t, imag_t = real.T, imag.T
+        chans.append((real, imag, real.T, imag.T))
+
+    def mirror(chan, kind, corner):
+        corner = corner.T
+        out_ref[chan, kind, half:, 0:half] = -corner if kind else corner
+
+    waiting = None
+    for chan, (real, imag, real_t, imag_t) in enumerate(chans):
         right = jnp.concatenate([real, imag], axis=0)
-        for kind, left in enumerate(
-            [
-                jnp.concatenate([real_t, imag_t], axis=1),
-                jnp.concatenate([imag_t, -real_t], axis=1),
-            ]
-        ):
+        for kind in range(2):
+            left = jnp.concatenate([imag_t, -real_t] if kind else [real_t, imag_t], axis=1)
             upper = jnp.dot(left[:half], right, preferred_element_type=jnp.float32) * scale
-            corner = upper[:, half:].T
             out_ref[chan, kind, 0:half, :] = upper
-            out_ref[chan, kind, half:, 0:half] = -corner if kind else corner
+            if waiting is not None:
+                mirror(*waiting)
+            waiting = (chan, kind, upper[:, half:])
             out_ref[chan, kind, half:, half:] = (
                 jnp.dot(left[half:], right[:, half:], preferred_element_type=jnp.float32) * scale
             )
+    mirror(*waiting)
 
 
 def correlate(arrived, n_inp, late_chans, late=(), before=None):

time: 398 us -> 398 us (level)
  no operation moved by 1% of the time
where the time goes in v5:
time: 398 us; the launch traced here: 395 us
  Pallas kernels  393 us (99%)
    pallas_call x1, Pallas kernels, spread(): pl.pallas_call(functools.partial(spread_kernel, n_inp, n_time), out_shape...  366 us
    pallas_call x2, Pallas kernels, correlate(): pl.pallas_call(body, grid=(turns,), out_shape=jax.ShapeDtypeStruct((count...  26.4 us
  transfers between devices with their start and end apart: 2, of which 1 were waited for; matrix products, arithmetic and copies ran while one was open for 0% of the time, Pallas kernels for 4%

profile of v5, /device:TPU:16, one launch (start us, length us, event | category | flops | bytes accessed | tf_op | source)
XLA Modules:
  0.0 394.8 jit_solution(4051914148824500257)
XLA Ops:
  0.0 366.3 %filter_transform_spread.1 = (bf16[32,32,64,128]{3,2,1,0:T(8,128)(2,1)}, bf16[12,64,128]{2,1,0:T(8,128)(2,1)}, bf16[12,64,128]{2,1,0:T(8,128)(2,1)}) custom-call(bf16[128,64,1024]{2,1,0:T(8,128)(2,1)} %x_hbm.1, f32[512,128]{1,0:T(8,128)} %gain_ref.1, bf16[1024,1024]{1,0:T(8,128)(2,1)} %constant.4.clone.table_ref, f32[4,1024]{1,0:T(4,128)} %constant.5.clone.window_ref), custom_call_target="tpu_custom_call" | custom-call | flops 17179869184 | bytes 33554432 | tf_op jit(solution)/shard_map/filter_transform_spread/pallas_call | solution.py:335
  366.3 0.1 collective-permute-start
  366.4 0.1 collective-permute-start.1
  366.4 15.7 %correlate_first.1.refs_3_ = f32[16,2,512,512]{3,2,1,0:T(8,128)} custom-call(bf16[32,32,64,128]{3,2,1,0:T(8,128)(2,1)} %get-tuple-element.8.block_ref.refs_0_), custom_call_target="tpu_custom_call" | custom-call | flops 8053063680 | bytes 31457280 | tf_op jit(solution)/shard_map/correlate_first/pallas_call | solution.py:444
  382.2 0.0 collective-permute-done.refs_1_
  382.2 2.0 collective-permute-done.1.refs_2_
  384.1 10.7 %correlate_second.1 = f32[16,2,512,512]{3,2,1,0:T(8,128)} custom-call(bf16[32,32,64,128]{3,2,1,0:T(8,128)(2,1)} %get-tuple-element.8.block_ref.refs_0_, bf16[12,64,128]{2,1,0:T(8,128)(2,1)S(1)} %collective-permute-done.refs_1_, bf16[12,64,128]{2,1,0:T(8,128)(2,1)S(1)} %collective-permute-done.1.refs_2_, ...), custom_call_target="tpu_custom_call", output_to_operand_aliasing={{}: (3, {})} | custom-call | flops 4831838208 | bytes 18874368 | tf_op jit(solution)/shard_map/correlate_second/pallas_call | solution.py:444
Async XLA Ops:
  366.3 15.9 %collective-permute-start = (bf16[12,64,128]{2,1,0:T(8,128)(2,1)}, bf16[12,64,128]{2,1,0:T(8,128)(2,1)S(1)}, u32[]{:S(2)}, u32[]{:S(2)}) collective-permute-start(bf16[12,64,128]{2,1,0:T(8,128)(2,1)} %get-tuple-element.9), channel_id=1, source_target_pairs={{0,16},{8,24},{16,0},{24,8},{1,17},{9,25},{17,1},{25,9},{2,18},{10... | collective-permute-start | bytes 589832 | tf_op jit(solution)/shard_map/ppermute | solution.py:469
  366.4 17.8 %collective-permute-start.1 = (bf16[12,64,128]{2,1,0:T(8,128)(2,1)}, bf16[12,64,128]{2,1,0:T(8,128)(2,1)S(1)}, u32[]{:S(2)}, u32[]{:S(2)}) collective-permute-start(bf16[12,64,128]{2,1,0:T(8,128)(2,1)} %get-tuple-element.10), channel_id=1, source_target_pairs={{0,24},{8,16},{16,8},{24,0},{1,25},{9,17},{17,9},{25,1},{2,26},{10... | collective-permute-start | bytes 589832 | tf_op jit(solution)/shard_map/ppermute | solution.py:470
